TPU v7x, 256 devices: a whole 4x4x8 slice. The times are simulated.
256 devices in a mesh: rows: 32 (over x, z_hi, core), dp: 8 (over z_lo, y).
Axes of the slice: x: 4, y: 4, z: 8 (z_hi: 4, z_lo: 2; z = z_hi * 2 + z_lo), core: 2. Of those that a mesh axis runs over, the one named last changes fastest.
Arguments:
- inputs: bfloat16 [8, 128, 128, 768], P('dp', 'rows')
- cotangent: bfloat16 [8, 128, 128, 768], P('dp', 'rows'), may hold values from -6 to 6
- extents: int32 [8, 2], P('dp'), may hold values from 4 to 128, as said below
- weights: bfloat16 [768, 3072], P('dp')
Outputs:
- outputs: bfloat16 [8, 128, 128, 768], P('dp', 'rows')
- input_grads: bfloat16 [8, 128, 128, 768], P('dp', 'rows')
- weight_grads: float32 [768, 3072], P('dp')
Inputs may be any that keep to these rules, and one draw needn't show every extreme that they name: `extents`: column 0 is a valid height of at least 4, column 1 a valid width of at least 16; some image is valid in full.
All inputs are finite; a program needn't handle non-finite values.
Results may differ from a plain program's by a relative error of at most 0.034.
Values may be sent and summed in bfloat16 or wider, within the bound.
A program may use at most 128 MiB of HBM per device.

v0:
```python
import jax
import jax.numpy as jnp
from jax import lax
from jax.sharding import PartitionSpec as P

HEADS = 24
HEAD_DIM = 32
GRID_COLS = 8


epsilon = 1e-05


def normalize(tokens):
    widened = tokens.astype(jnp.float32)
    centered = widened - jnp.mean(widened, axis=-1, keepdims=True)
    inv_std = lax.rsqrt(jnp.mean(centered * centered, axis=-1, keepdims=True) + epsilon)
    return (centered * inv_std, inv_std)


def outbound(values, rows_count):
    height_dev, strip, channels = values.shape
    col_groups = strip // GRID_COLS
    shuffled = values.reshape(height_dev, GRID_COLS, col_groups, channels).transpose(0, 2, 1, 3)
    return shuffled.reshape(
        rows_count, height_dev * col_groups // rows_count, 1, GRID_COLS, channels
    )


def inbound(values, height_dev, strip):
    channels = values.shape[-1]
    col_groups = strip // GRID_COLS
    shuffled = values.reshape(height_dev, col_groups, GRID_COLS, channels).transpose(0, 2, 1, 3)
    return shuffled.reshape(height_dev * strip, channels)


def local_valid(extent, rows_at, height_dev, strip):
    row_ids = rows_at * height_dev + lax.broadcasted_iota(jnp.int32, (height_dev, strip), 0)
    col_ids = lax.broadcasted_iota(jnp.int32, (height_dev, strip), 1)
    return jnp.logical_and(row_ids < extent[0], col_ids < extent[1]).reshape(-1)


def group_valid(extent, rows_at, height_dev, strip, rows_count):
    col_groups = strip // GRID_COLS
    group_count = height_dev * col_groups // rows_count
    shape = (group_count, rows_count, GRID_COLS)
    group_ids = rows_at * group_count + lax.broadcasted_iota(jnp.int32, shape, 0)
    row_ids = group_ids // col_groups + height_dev * lax.broadcasted_iota(jnp.int32, shape, 1)
    col_ids = lax.broadcasted_iota(jnp.int32, shape, 2) * col_groups + group_ids % col_groups
    valid = jnp.logical_and(row_ids < extent[0], col_ids < extent[1])
    return valid.reshape(group_count, rows_count * GRID_COLS)


def split_heads(values):
    group_count, members, _ = values.shape
    return values.reshape(group_count, members, HEADS, HEAD_DIM)


def probabilities(queries, key_vecs, key_valid):
    scores = jnp.einsum(
        "gmhe,gnhe->ghmn",
        split_heads(queries),
        split_heads(key_vecs),
        preferred_element_type=jnp.float32,
    ) * HEAD_DIM ** (-0.5)
    scores = jnp.where(key_valid[:, None, None, :], scores, -jnp.inf)
    top_score = jnp.max(scores, axis=-1, keepdims=True)
    shifted = jnp.exp(scores - top_score)
    return shifted / jnp.sum(shifted, axis=-1, keepdims=True)


def attend(queries, key_vecs, value_vecs, key_valid):
    chances = probabilities(queries, key_vecs, key_valid).astype(jnp.bfloat16)
    attended = jnp.einsum(
        "ghmn,gnhe->gmhe", chances, split_heads(value_vecs), preferred_element_type=jnp.float32
    )
    return attended.astype(jnp.bfloat16).reshape(queries.shape)


def attend_back(queries, key_vecs, value_vecs, key_valid, out_grad):
    chances = probabilities(queries, key_vecs, key_valid)
    chances_low = chances.astype(jnp.bfloat16)
    grad_heads = split_heads(out_grad)
    chance_grad = jnp.einsum(
        "gmhe,gnhe->ghmn", grad_heads, split_heads(value_vecs), preferred_element_type=jnp.float32
    )
    value_grad = jnp.einsum(
        "ghmn,gmhe->gnhe", chances_low, grad_heads, preferred_element_type=jnp.float32
    )
    spread = jnp.sum(chances * chance_grad, axis=-1, keepdims=True)
    score_grad = (chances * (chance_grad - spread) * HEAD_DIM ** (-0.5)).astype(jnp.bfloat16)
    query_grad = jnp.einsum(
        "ghmn,gnhe->gmhe", score_grad, split_heads(key_vecs), preferred_element_type=jnp.float32
    )
    key_grad = jnp.einsum(
        "ghmn,gmhe->gnhe", score_grad, split_heads(queries), preferred_element_type=jnp.float32
    )
    shape = queries.shape
    return (
        query_grad.astype(jnp.bfloat16).reshape(shape),
        key_grad.astype(jnp.bfloat16).reshape(shape),
        value_grad.astype(jnp.bfloat16).reshape(shape),
    )


def finish(normed, unit_rows, inv_std, proj_grad, attended, masked_grad, in_weights):
    unit_grad = lax.dot_general(
        proj_grad, in_weights, (((1,), (1,)), ((), ())), preferred_element_type=jnp.float32
    )
    input_grads = masked_grad.astype(jnp.float32) + inv_std * (
        unit_grad
        - jnp.mean(unit_grad, axis=-1, keepdims=True)
        - unit_rows * jnp.mean(unit_grad * unit_rows, axis=-1, keepdims=True)
    )
    contract = (((0,), (0,)), ((), ()))
    terms = lax.psum_scatter(
        jnp.concatenate(
            [
                lax.dot_general(normed, proj_grad, contract, preferred_element_type=jnp.float32),
                lax.dot_general(
                    attended, masked_grad, contract, preferred_element_type=jnp.float32
                ),
            ],
            axis=1,
        ).astype(jnp.bfloat16),
        "dp",
        scatter_dimension=0,
        tiled=True,
    )
    weight_grads = lax.psum(terms, "rows").astype(jnp.float32)
    return (input_grads.astype(jnp.bfloat16), weight_grads)


def per_device(inputs, cotangent, extents, weights):
    rows_count = lax.axis_size("rows")
    rows_at = lax.axis_index("rows")
    full_weights = lax.all_gather(weights, "dp", axis=0, tiled=True)
    width = full_weights.shape[0]
    in_weights = full_weights[:, : 3 * width]
    out_weights = full_weights[:, 3 * width :]
    image = inputs[0]
    grad_image = cotangent[0]
    extent = extents[0]
    height_dev, strip, _ = image.shape
    group_keys = group_valid(extent, rows_at, height_dev, strip, rows_count)
    group_count = group_keys.shape[0]

    def regroup(values):
        return values.reshape(1, group_count, rows_count, GRID_COLS, width)

    def grouped(values):
        return values.reshape(group_count, -1, width)

    tokens_in = image.reshape(-1, width)
    home_valid = local_valid(extent, rows_at, height_dev, strip)
    masked_grad = grad_image.reshape(-1, width) * home_valid[:, None].astype(jnp.bfloat16)
    unit_rows, inv_std = normalize(tokens_in)
    normed = unit_rows.astype(jnp.bfloat16)
    projected = jnp.dot(normed, in_weights, preferred_element_type=jnp.float32).astype(jnp.bfloat16)

    def send_out(values):
        return outbound(values.reshape(height_dev, strip, width), rows_count)

    arrived = (
        lax.all_to_all(
            send_out(projected[:, :width]), "rows", split_axis=0, concat_axis=2, tiled=True
        ),
        lax.all_to_all(
            send_out(projected[:, width : 2 * width]),
            "rows",
            split_axis=0,
            concat_axis=2,
            tiled=True,
        ),
        lax.all_to_all(
            send_out(projected[:, 2 * width :]), "rows", split_axis=0, concat_axis=2, tiled=True
        ),
    )
    queries = grouped(arrived[0])
    key_vecs = grouped(arrived[1])
    value_vecs = grouped(arrived[2])
    attended_groups = attend(queries, key_vecs, value_vecs, group_keys)
    returned = lax.all_to_all(
        regroup(attended_groups), "rows", split_axis=2, concat_axis=0, tiled=True
    )
    attended = inbound(returned, height_dev, strip)
    final_out = (
        tokens_in.astype(jnp.float32)
        + jnp.dot(attended, out_weights, preferred_element_type=jnp.float32)
    ).astype(jnp.bfloat16)
    out_grad = lax.dot_general(
        masked_grad, out_weights, (((1,), (1,)), ((), ())), preferred_element_type=jnp.float32
    ).astype(jnp.bfloat16)
    grad_groups = grouped(
        lax.all_to_all(send_out(out_grad), "rows", split_axis=0, concat_axis=2, tiled=True)
    )
    query_grad, key_grad, value_grad = attend_back(
        queries, key_vecs, value_vecs, group_keys, grad_groups
    )
    grads_home = (
        lax.all_to_all(regroup(query_grad), "rows", split_axis=2, concat_axis=0, tiled=True),
        lax.all_to_all(regroup(key_grad), "rows", split_axis=2, concat_axis=0, tiled=True),
        lax.all_to_all(regroup(value_grad), "rows", split_axis=2, concat_axis=0, tiled=True),
    )
    proj_grad = jnp.concatenate(
        [
            inbound(grads_home[0], height_dev, strip),
            inbound(grads_home[1], height_dev, strip),
            inbound(grads_home[2], height_dev, strip),
        ],
        axis=1,
    )
    final_in, weight_grads = finish(
        normed, unit_rows, inv_std, proj_grad, attended, masked_grad, in_weights
    )
    return (
        final_out.reshape(1, height_dev, strip, width),
        final_in.reshape(1, height_dev, strip, width),
        weight_grads,
    )


def solution(mesh):
    placed = (
        P("dp", "rows", None, None),
        P("dp", "rows", None, None),
        P("dp", None),
        P("dp", None),
    )
    return jax.shard_map(
        per_device,
        mesh=mesh,
        in_specs=placed,
        out_specs=(P("dp", "rows", None, None), P("dp", "rows", None, None), P("dp", None)),
        check_vma=False,
    )
```

profile of v0, /device:TPU:57, one launch (start us, length us, event | category | flops | bytes accessed | tf_op | source)
XLA Modules:
  0.0 727.7 jit_solution(3369059329500954813)
XLA Ops:
  13.2 56.2 %all-gather.2.cloned.1.call-done = bf16[768,3072]{1,0:T(8,128)(2,1)} async-done(((bf16[96,3072]{1,0:T(8,128)(2,1)}), bf16[768,3072]{1,0:T(8,128)(2,1)}) %all-gather.2.cloned.1.call-update) | async-done | bytes 4718608 | tf_op jit(solution)/shard_map/all_gather | solution.py:137
  72.6 9.8 %all-to-all-start.4 = ((bf16[32,2,1,8,768]{4,3,1,2,0:T(8,128)(2,1)}), bf16[32,2,1,8,768]{4,3,1,2,0:T(8,128)(2,1)S(1)}, u32[]{:S(2)}, u32[]{:S(2)}) async-start(bf16[32,2,1,8,768]{4,3,1,2,0:T(8,128)(2,1)} %bitcast.35), calls=%async_computation.4 | async-start | bytes 1572864 | tf_op jit(solution)/shard_map/all_to_all | solution.py:195
  88.7 18.2 %all-to-all-done.4 = bf16[32,2,1,8,768]{4,3,1,2,0:T(8,128)(2,1)S(1)} async-done(((bf16[32,2,1,8,768]{4,3,1,2,0:T(8,128)(2,1)}), bf16[32,2,1,8,768]{4,3,1,2,0:T(8,128)(2,1)S(1)}, u32[]{:S(2)}, u32[]{:S(2)}) %all-to-all-start.4) | async-done | bytes 786464 | tf_op jit(solution)/shard_map/all_to_all | solution.py:195
  112.6 22.4 %all-to-all-done.1 = bf16[32,2,1,8,768]{4,3,1,2,0:T(8,128)(2,1)} async-done(((bf16[32,2,1,8,768]{4,3,1,2,0:T(8,128)(2,1)}), bf16[32,2,1,8,768]{4,3,1,2,0:T(8,128)(2,1)}, u32[]{:S(2)}, u32[]{:S(2)}) %all-to-all-start.1) | async-done | bytes 786464 | tf_op jit(solution)/shard_map/all_to_all | solution.py:165
  140.5 22.2 %all-to-all-done.2 = bf16[32,2,1,8,768]{4,3,1,2,0:T(8,128)(2,1)S(1)} async-done(((bf16[32,2,1,8,768]{4,3,1,2,0:T(8,128)(2,1)}), bf16[32,2,1,8,768]{4,3,1,2,0:T(8,128)(2,1)S(1)}, u32[]{:S(2)}, u32[]{:S(2)}) %all-to-all-start.2) | async-done | bytes 786464 | tf_op jit(solution)/shard_map/all_to_all | solution.py:168
  162.8 5.1 all-to-all-start
  170.4 4.7 reshape_reshape.49
  181.8 9.1 %all-to-all-done = bf16[32,2,1,8,768]{4,3,1,2,0:T(8,128)(2,1)S(1)} async-done(((bf16[32,2,1,8,768]{4,3,1,2,0:T(8,128)(2,1)}), bf16[32,2,1,8,768]{4,3,1,2,0:T(8,128)(2,1)S(1)}, u32[]{:S(2)}, u32[]{:S(2)}) %all-to-all-start) | async-done | bytes 786464 | tf_op jit(solution)/shard_map/all_to_all | solution.py:175
  197.7 5.0 reshape_reshape.46
  213.8 11.1 %fusion.75 = (f32[2,24,256]{2,1,0:T(8,128)S(1)}, f32[2,24,256,256]{2,3,1,0:T(8,128)}) fusion(pred[2,256]{1,0:T(4,128)(4,1)S(1)} %compare_and_fusion, bf16[2,256,24,32]{1,3,2,0:T(8,128)(2,1)S(1)} %copy.54, bf16[2,256,24,32]{1,3,2,0:T(8,128)(2,1)} %copy.55), kind=kOutput, calls=%fused_computation.87 | convolution fusion | flops 213909760 | bytes 14205440 | tf_op jit(solution)/shard_map/sub | solution.py:68
  224.9 5.8 fusion.57
  243.2 7.4 %fusion.54 = bf16[2,256,24,32]{1,3,2,0:T(8,128)(2,1)} fusion(bf16[2,256,24,32]{1,3,2,0:T(8,128)(2,1)S(1)} %copy.64, f32[2,24,256,256]{2,3,1,0:T(8,128)} %get-tuple-element.15, f32[2,24,256]{2,1,0:T(8,128)S(1)} %get-tuple-element.14), kind=kOutput, calls=%fused_computation.50 | convolution fusion | flops 208011264 | bytes 14204928 | tf_op jit(solution)/shard_map/ghmn,gmhe->gnhe/dot_general | solution.py:87
  259.8 6.8 all-to-all-done.3
  266.5 4.7 all-to-all-start.7
  271.3 7.4 %fusion.76 = f32[2,24,256,256]{2,3,1,0:T(8,128)} fusion(bf16[2,256,24,32]{1,3,2,0:T(8,128)(2,1)S(1)} %copy-done.3, bf16[2,256,24,32]{1,3,2,0:T(8,128)(2,1)} %copy-done.4), kind=kOutput, calls=%fused_computation.88 | convolution fusion | flops 201326592 | bytes 14155776 | tf_op jit(solution)/shard_map/gmhe,gnhe->ghmn/dot_general | solution.py:84
  278.7 17.5 %fusion.48 = bf16[2,256,24,32]{1,3,2,0:T(8,128)(2,1)S(1)} fusion(bf16[2,256,24,32]{1,3,2,0:T(8,128)(2,1)} %copy-done.12, f32[2,24,256,256]{2,3,1,0:T(8,128)} %fusion.76, f32[2,24,256,256]{2,3,1,0:T(8,128)} %get-tuple-element.15, f32[2,24,256]{2,1,0:T(8,128)S(1)} %get-tuple-element.14), kind=kOutput, calls=%fused_computation.48 | convolution fusion | flops 223752448 | bytes 26787840 | tf_op jit(solution)/shard_map/ghmn,gmhe->gnhe/dot_general | solution.py:95
  304.2 9.9 %all-to-all-start.6 = ((bf16[1,2,32,8,768]{4,3,1,0,2:T(8,128)(2,1)}), bf16[1,2,32,8,768]{4,3,1,0,2:T(8,128)(2,1)}, u32[]{:S(2)}, u32[]{:S(2)}) async-start(bf16[1,2,32,8,768]{4,3,1,0,2:T(8,128)(2,1)} %copy.74), calls=%async_computation.6 | async-start | bytes 1572864 | tf_op jit(solution)/shard_map/all_to_all | solution.py:202
  314.2 18.5 %fusion.51 = bf16[2,256,24,32]{1,3,2,0:T(8,128)(2,1)} fusion(bf16[2,256,24,32]{1,3,2,0:T(8,128)(2,1)} %copy.55, f32[2,24,256,256]{2,3,1,0:T(8,128)} %fusion.76, f32[2,24,256,256]{2,3,1,0:T(8,128)} %get-tuple-element.15, f32[2,24,256]{2,1,0:T(8,128)S(1)} %get-tuple-element.14), kind=kOutput, calls=%fused_computation.49 | convolution fusion | flops 223752448 | bytes 26787840 | tf_op jit(solution)/shard_map/ghmn,gnhe->gmhe/dot_general | solution.py:92
  336.9 4.7 reshape_reshape.50
  343.7 9.8 %all-to-all-start.5 = ((bf16[1,2,32,8,768]{4,3,1,0,2:T(8,128)(2,1)}), bf16[1,2,32,8,768]{4,3,1,0,2:T(8,128)(2,1)}, u32[]{:S(2)}, u32[]{:S(2)}) async-start(bf16[1,2,32,8,768]{4,3,1,0,2:T(8,128)(2,1)} %copy.69), calls=%async_computation.5 | async-start | bytes 1572864 | tf_op jit(solution)/shard_map/all_to_all | solution.py:201
  359.1 17.6 %all-to-all-done.5 = bf16[1,2,32,8,768]{4,3,1,0,2:T(8,128)(2,1)} async-done(((bf16[1,2,32,8,768]{4,3,1,0,2:T(8,128)(2,1)}), bf16[1,2,32,8,768]{4,3,1,0,2:T(8,128)(2,1)}, u32[]{:S(2)}, u32[]{:S(2)}) %all-to-all-start.5) | async-done | bytes 786464 | tf_op jit(solution)/shard_map/all_to_all | solution.py:201
  389.5 4.9 fusion.72
  394.4 48.4 %reduce-scatter.2.cloned.1.call-done = bf16[96,3072]{1,0:T(8,128)(2,1)} async-done(((bf16[768,3072]{1,0:T(8,128)(2,1)}), bf16[96,3072]{1,0:T(8,128)(2,1)}) %reduce-scatter.2.cloned.1.call-update) | async-done | bytes 589840 | tf_op jit(solution)/shard_map/reduce_scatter | solution.py:116
  444.3 274.4 %all-reduce.2.cloned.1.call-done = bf16[96,3072]{1,0:T(8,128)(2,1)} async-done(((bf16[96,3072]{1,0:T(8,128)(2,1)}), bf16[96,3072]{1,0:T(8,128)(2,1)}) %all-reduce.2.cloned.1.call-update) | async-done | bytes 589840 | tf_op jit(solution)/shard_map/psum | solution.py:130
  (98 shorter events, 111.5 us)
Async XLA Ops:
  7.2 62.2 %all-gather.2.cloned.1.call-start = ((), (), s32[]{:S(2)}) async-start(), calls=%async_computation.9 | async-start | bytes 5308416 | tf_op jit(solution)/shard_map/all_gather | solution.py:137
  7.9 74.5 %copy-start = (bf16[1,4,128,768]{3,2,1,0:T(8,128)(2,1)S(1)}, bf16[1,4,128,768]{3,2,1,0:T(8,128)(2,1)}, u32[]{:S(2)}) copy-start(bf16[1,4,128,768]{3,2,1,0:T(8,128)(2,1)} %param.4) | copy-start | bytes 2359300
  72.6 34.3 %all-to-all-start.4 = ((bf16[32,2,1,8,768]{4,3,1,2,0:T(8,128)(2,1)}), bf16[32,2,1,8,768]{4,3,1,2,0:T(8,128)(2,1)S(1)}, u32[]{:S(2)}, u32[]{:S(2)}) async-start(bf16[32,2,1,8,768]{4,3,1,2,0:T(8,128)(2,1)} %bitcast.35), calls=%async_computation.4 | async-start | bytes 1572864 | tf_op jit(solution)/shard_map/all_to_all | solution.py:195
  83.1 4.3 copy-start.6
  106.9 28.2 %all-to-all-start.1 = ((bf16[32,2,1,8,768]{4,3,1,2,0:T(8,128)(2,1)}), bf16[32,2,1,8,768]{4,3,1,2,0:T(8,128)(2,1)}, u32[]{:S(2)}, u32[]{:S(2)}) async-start(bf16[32,2,1,8,768]{4,3,1,2,0:T(8,128)(2,1)} %bitcast.164), calls=%async_computation.1 | async-start | bytes 1572864 | tf_op jit(solution)/shard_map/all_to_all | solution.py:165
  135.1 27.7 %all-to-all-start.2 = ((bf16[32,2,1,8,768]{4,3,1,2,0:T(8,128)(2,1)}), bf16[32,2,1,8,768]{4,3,1,2,0:T(8,128)(2,1)S(1)}, u32[]{:S(2)}, u32[]{:S(2)}) async-start(bf16[32,2,1,8,768]{4,3,1,2,0:T(8,128)(2,1)} %bitcast.163), calls=%async_computation.2 | async-start | bytes 1572864 | tf_op jit(solution)/shard_map/all_to_all | solution.py:168
  162.8 28.2 %all-to-all-start = ((bf16[32,2,1,8,768]{4,3,1,2,0:T(8,128)(2,1)}), bf16[32,2,1,8,768]{4,3,1,2,0:T(8,128)(2,1)S(1)}, u32[]{:S(2)}, u32[]{:S(2)}) async-start(bf16[32,2,1,8,768]{4,3,1,2,0:T(8,128)(2,1)} %bitcast.160), calls=%async_computation | async-start | bytes 1572864 | tf_op jit(solution)/shard_map/all_to_all | solution.py:175
  178.6 64.6 %copy-start.2 = (bf16[2,256,24,32]{1,3,2,0:T(8,128)(2,1)}, bf16[2,256,24,32]{1,3,2,0:T(8,128)(2,1)S(1)}, u32[]{:S(2)}) copy-start(bf16[2,256,24,32]{1,3,2,0:T(8,128)(2,1)S(1)} %copy.64) | copy-start | bytes 2359300
  197.7 27.2 %copy-start.4 = (bf16[2,256,24,32]{1,3,2,0:T(8,128)(2,1)}, bf16[2,256,24,32]{1,3,2,0:T(8,128)(2,1)S(1)}, u32[]{:S(2)}) copy-start(bf16[2,256,24,32]{1,3,2,0:T(8,128)(2,1)S(1)} %copy.56) | copy-start | bytes 2359300
  197.7 9.2 %copy-start.5 = (bf16[1,2,32,1,8,768]{5,4,2,1,3,0:T(8,128)(2,1)S(1)}, bf16[1,2,32,1,8,768]{5,4,2,1,3,0:T(8,128)(2,1)}, u32[]{:S(2)}) copy-start(bf16[1,2,32,1,8,768]{5,4,2,1,3,0:T(8,128)(2,1)} %copy.50) | copy-start | bytes 2359300
  213.8 11.1 %copy-start.12 = (bf16[2,256,24,32]{1,3,2,0:T(8,128)(2,1)}, bf16[2,256,24,32]{1,3,2,0:T(8,128)(2,1)S(1)}, u32[]{:S(2)}) copy-start(bf16[2,256,24,32]{1,3,2,0:T(8,128)(2,1)S(1)} %copy.54) | copy-start | bytes 2359300
  238.8 27.7 %all-to-all-start.3 = ((bf16[1,2,32,8,768]{4,3,1,0,2:T(8,128)(2,1)}), bf16[1,2,32,8,768]{4,3,1,0,2:T(8,128)(2,1)S(1)}, u32[]{:S(2)}, u32[]{:S(2)}) async-start(bf16[1,2,32,8,768]{4,3,1,0,2:T(8,128)(2,1)} %copy.59), calls=%async_computation.3 | async-start | bytes 1572864 | tf_op jit(solution)/shard_map/all_to_all | solution.py:183
  250.6 20.7 %copy-start.3 = (bf16[2,256,24,32]{1,3,2,0:T(8,128)(2,1)S(1)}, bf16[2,256,24,32]{1,3,2,0:T(8,128)(2,1)}, u32[]{:S(2)}) copy-start(bf16[2,256,24,32]{1,3,2,0:T(8,128)(2,1)} %copy-done.2) | copy-start | bytes 2359300
  266.5 37.7 %all-to-all-start.7 = ((bf16[1,2,32,8,768]{4,3,1,0,2:T(8,128)(2,1)}), bf16[1,2,32,8,768]{4,3,1,0,2:T(8,128)(2,1)S(1)}, u32[]{:S(2)}, u32[]{:S(2)}) async-start(bf16[1,2,32,8,768]{4,3,1,0,2:T(8,128)(2,1)} %copy.79), calls=%async_computation.7 | async-start | bytes 1572864 | tf_op jit(solution)/shard_map/all_to_all | solution.py:203
  304.2 39.5 %all-to-all-start.6 = ((bf16[1,2,32,8,768]{4,3,1,0,2:T(8,128)(2,1)}), bf16[1,2,32,8,768]{4,3,1,0,2:T(8,128)(2,1)}, u32[]{:S(2)}, u32[]{:S(2)}) async-start(bf16[1,2,32,8,768]{4,3,1,0,2:T(8,128)(2,1)} %copy.74), calls=%async_computation.6 | async-start | bytes 1572864 | tf_op jit(solution)/shard_map/all_to_all | solution.py:202
  332.6 21.2 %copy-start.1 = (bf16[1,4,128,768]{3,2,1,0:T(8,128)(2,1)S(1)}, bf16[1,4,128,768]{3,2,1,0:T(8,128)(2,1)}, u32[]{:S(2)}) copy-start(bf16[1,4,128,768]{3,2,1,0:T(8,128)(2,1)} %param.5) | copy-start | bytes 2359300
  343.7 33.1 %all-to-all-start.5 = ((bf16[1,2,32,8,768]{4,3,1,0,2:T(8,128)(2,1)}), bf16[1,2,32,8,768]{4,3,1,0,2:T(8,128)(2,1)}, u32[]{:S(2)}, u32[]{:S(2)}) async-start(bf16[1,2,32,8,768]{4,3,1,0,2:T(8,128)(2,1)} %copy.69), calls=%async_computation.5 | async-start | bytes 1572864 | tf_op jit(solution)/shard_map/all_to_all | solution.py:201
  353.5 89.3 %reduce-scatter.2.cloned.1.call-start = ((), (), s32[]{:S(2)}) async-start(), calls=%async_computation.10 | async-start | bytes 5308416 | tf_op jit(solution)/shard_map/reduce_scatter | solution.py:116
  355.8 24.7 %copy-start.7 = (bf16[512,768]{1,0:T(8,128)(2,1)S(1)}, bf16[512,768]{1,0:T(8,128)(2,1)}, u32[]{:S(2)}) copy-start(bf16[512,768]{1,0:T(8,128)(2,1)} %copy-done.6) | copy-start | bytes 2359300
  356.9 23.7 %copy-start.8 = (bf16[4,8,16,768]{3,2,1,0:T(8,128)(2,1)S(1)}, bf16[4,8,16,768]{3,2,1,0:T(8,128)(2,1)}, u32[]{:S(2)}) copy-start(bf16[4,8,16,768]{3,2,1,0:T(8,128)(2,1)} %copy.80) | copy-start | bytes 2359300
  376.7 3.8 copy-start.9
  378.1 4.6 copy-start.11
  385.4 1.1 copy-start.10
  385.4 333.3 %all-reduce.2.cloned.1.call-start = ((), (), s32[]{:S(2)}) async-start(), calls=%async_computation.11 | async-start | bytes 1179648 | tf_op jit(solution)/shard_map/psum | solution.py:130
Sparse Core Ops, SparseCore 0:
  9.8 59.5 all-gather.1
  385.6 57.1 reduce-scatter.1
  445.4 273.2 all-reduce.1
where the time goes:
time: 738 us; the launch traced here: 728 us
  waiting for transfers between devices  476 us (64%)
  matrix products  86.4 us (12%)
  local copies, waits for them, and re-layouts  84.3 us (11%)
  starting transfers between devices  53.1 us (7%)
  between operations  14.4 us (2%)
  other arithmetic  13.4 us (2%)
    psum x1, waiting for transfers between devices, finish(): weight_grads = lax.psum(terms, 'rows').astype(jnp.float32)  274 us
    all_gather x1, waiting for transfers between devices, per_device(): full_weights = lax.all_gather(weights, 'dp', axis=0, tiled=True)  56.2 us
    reduce_scatter x1, waiting for transfers between devices, finish(): lax.psum_scatter(jnp.concatenate([lax.dot_general(normed, proj_grad, cont...  48.4 us
    another operation x8, local copies, waits for them, and re-layouts, split_heads(): return values.reshape(group_count, members, HEADS, HEAD_DIM)  30.8 us
    all_to_all x1, waiting for transfers between devices, per_device(): lax.all_to_all(send_out(projected[:, :width]), 'rows', split_axis=0, conc...  22.4 us
    all_to_all x1, waiting for transfers between devices, per_device(): lax.all_to_all(send_out(projected[:, width:2 * width]), 'rows', split_axi...  22.2 us
    another operation x8, local copies, waits for them, and re-layouts, regroup(): return values.reshape(1, group_count, rows_count, GRID_COLS, width)  21.5 us
    dot_general x1, matrix products, attend_back(): jnp.einsum('ghmn,gnhe->gmhe', score_grad, split_heads(key_vecs), preferre...  18.5 us
  transfers between devices with their start and end apart: 11, of which 9 were waited for; matrix products, arithmetic and copies ran while one was open for 17% of the time, Pallas kernels for 0%

commit v1 on v0

v1 whole, which is shorter than its diff:
```python
import math

import jax
import jax.numpy as jnp
from jax import lax
from jax.experimental import pallas as pl
from jax.experimental.pallas import tpu as pltpu
from jax.sharding import PartitionSpec as P

MESH = pl.DeviceIdType.MESH
BF16 = jnp.bfloat16
F32 = jnp.float32

D = 768
HEADS = 24
HEAD_DIM = 32
TOKENS = 512
MEMBERS = 256
HALF = 384
ROOT = HEAD_DIM ** (-0.5)
EPSILON = 1e-05

CONTRACT_LAST = (((1,), (1,)), ((), ()))


def dot(a, b):
    return jnp.dot(a, b, preferred_element_type=F32)


def dot_last(a, b):
    return lax.dot_general(a, b, CONTRACT_LAST, preferred_element_type=F32)


def split(block):
    wide = block.astype(F32).reshape(8, 16, block.shape[-1])
    return [wide[:, 8 * g : 8 * g + 8, :].reshape(64, block.shape[-1]) for g in range(2)]


def merge(first, second):
    parts = [p.reshape(8, 8, p.shape[-1]) for p in (first, second)]
    return jnp.concatenate(parts, axis=1).reshape(128, first.shape[-1])


def kernel(
    extent_ref,
    x_ref,
    g_ref,
    w_ref,
    out_ref,
    ig_ref,
    wg_ref,
    sent,
    came,
    weights,
    unit,
    inv,
    normed_t,
    qkv,
    kv_t,
    bias,
    chances,
    att_t,
    att,
    masked,
    out_grad,
    proj_grad,
    wide,
    terms,
    core_in,
    core_sum,
    y_in,
    y_sum,
    x_in,
    x_sum,
    z_in,
    total,
    whole,
    a_send,
    a_recv,
    w_send,
    w_recv,
    r_send,
    r_recv,
):
    rows_at = lax.axis_index("rows")
    dp_at = lax.axis_index("dp")
    x_at, zh, core = rows_at // 8, (rows_at // 2) % 4, rows_at % 2
    zl, y_at = dp_at // 4, dp_at % 4

    def device(x=None, h=None, c=None, l=None, y=None):
        x = x_at if x is None else x
        h = zh if h is None else h
        c = core if c is None else c
        l = zl if l is None else l
        y = y_at if y is None else y
        return (x * 8 + h * 2 + c, l * 4 + y)

    def push(src, dst, send, recv, to):
        pltpu.make_async_remote_copy(
            src_ref=src, dst_ref=dst, send_sem=send, recv_sem=recv, device_id=to, device_id_type=MESH
        ).start()

    def wait(ref, sem):
        pltpu.make_async_copy(ref, ref, sem).wait()

    def at16(i, size=16):
        return pl.ds(pl.multiple_of(i * 16, 16), size)

    for b in range(3):
        for n in range(3):
            weights[b, dp_at, :, pl.ds(n * 256, 256)] = w_ref[:, pl.ds(n * D + b * 256, 256)]
    weights[3, dp_at] = w_ref[:, pl.ds(3 * D, D)]
    barrier = pltpu.get_barrier_semaphore()

    @pl.loop(1, 32)
    def _(k):
        pl.semaphore_signal(
            barrier, inc=1, device_id=((rows_at + k) % 32, dp_at), device_id_type=MESH
        )

    @pl.loop(1, 8)
    def _(k):
        pl.semaphore_signal(
            barrier, inc=1, device_id=(rows_at, (dp_at + k) % 8), device_id_type=MESH
        )

    side = (zh + 3 + 2 * zl) % 4

    @pl.loop(1, 4)
    def _(k):
        for to in (
            device(x=(x_at + 1) % 4, y=(y_at + k) % 4),
            device(x=(x_at + 2) % 4, y=(y_at + k) % 4),
            device(x=(x_at + 3) % 4, y=(y_at + k) % 4),
            device(h=(zh + k) % 4, l=1 - zl),
            device(h=side, l=1 - zl, y=(y_at + k) % 4),
        ):
            pl.semaphore_signal(barrier, inc=1, device_id=to, device_id_type=MESH)

    to_row = lax.broadcasted_iota(jnp.int32, (128, 128), 0)
    from_row = lax.broadcasted_iota(jnp.int32, (128, 128), 1)
    gather = (from_row == (to_row % 8) * 16 + to_row // 8).astype(BF16)
    scatter = (from_row == (to_row % 16) * 8 + to_row // 16).astype(BF16)

    def reorder(matrix, src, dst):
        for i in range(4):
            part = pl.ds(128 * i, 128)
            dst[part, :] = dot(matrix, src[part, :]).astype(BF16)

    def exchange(t, part=0, first=1, last=32):
        @pl.loop(first, last)
        def _(k):
            kc, kx, kz = k // 16, (k // 4) % 4, k % 4
            peer = ((x_at + kx) % 4) * 8 + ((zh + kz) % 4) * 2 + (core + kc) % 2
            push(
                sent.at[t, at16(peer)],
                came.at[t, at16(rows_at)],
                a_send.at[t, part],
                a_recv.at[t],
                (peer, dp_at),
            )

        if part == 0:
            came[t, at16(rows_at), :] = sent[t, at16(rows_at), :]

    def left(t, part, count):
        wait(came.at[t, pl.ds(0, 16 * count)], a_send.at[t, part])

    def arrive(t):
        wait(came.at[t, pl.ds(0, 496)], a_recv.at[t])

    reorder(gather, x_ref, sent.at[0])
    pl.semaphore_wait(barrier, 53)

    piece = (pl.ds(pl.multiple_of((x_at // 2) * 48, 16), 48), pl.ds(pl.multiple_of((x_at % 2) * HALF, 128), HALF))
    near, far = pl.ds(zl * 4, 4), pl.ds((1 - zl) * 4, 4)

    def weights_far(p):
        mine = weights.at[2 * p + core, dp_at, piece[0], piece[1]]
        for k in range(4):
            to = device(h=zh if k < 2 else side, l=1 - zl, y=(y_at + k) % 4)
            push(mine, mine, w_send.at[p, 0], w_recv.at[p, 0], to)

    def weights_near(p):
        mine = weights.at[2 * p + core, dp_at]
        for k in range(1, 4):
            push(mine, mine, w_send.at[p, 1], w_recv.at[p, 1], device(y=(y_at + k) % 4))

    def weights_across(p):
        mine = weights.at[2 * p + core, far, piece[0], piece[1]]
        wait(mine, w_recv.at[p, 0])
        for k in range(1, 4):
            push(mine, mine, w_send.at[p, 2], w_recv.at[p, 2], device(x=(x_at + k) % 4))

    def weights_core_near(p):
        mine = weights.at[2 * p + core, near]
        wait(weights.at[2 * p, pl.ds(0, 3)], w_recv.at[p, 1])
        push(mine, mine, w_send.at[p, 3], w_recv.at[p, 3], device(c=1 - core))

    def weights_core_far(p):
        mine = weights.at[2 * p + core, far]
        wait(weights.at[2 * p, pl.ds(0, 3)], w_recv.at[p, 2])
        push(mine, mine, w_send.at[p, 4], w_recv.at[p, 4], device(c=1 - core))

    def weights_there(p):
        wait(weights.at[2 * p, near], w_recv.at[p, 3])
        wait(weights.at[2 * p, far], w_recv.at[p, 4])

    def weights_settle(p):
        wait(weights.at[2 * p, far, piece[0], piece[1]], w_send.at[p, 0])
        wait(weights.at[2 * p, pl.ds(0, 3)], w_send.at[p, 1])
        wait(weights.at[2 * p, pl.ds(0, 3)], w_send.at[p, 2])
        wait(weights.at[2 * p, near], w_send.at[p, 3])
        wait(weights.at[2 * p, far], w_send.at[p, 4])

    def block_weights(b):
        return weights[b].reshape(D, D)

    weights_far(0)
    weights_near(0)
    exchange(0)
    weights_across(0)
    weights_far(1)
    weights_near(1)
    reorder(gather, g_ref, sent.at[1])
    weights_core_near(0)
    weights_across(1)
    weights_core_far(0)
    weights_core_near(1)

    height, width = extent_ref[0, 0], extent_ref[0, 1]
    member = lax.broadcasted_iota(jnp.int32, (MEMBERS, 128), 0)
    row_ids = 4 * (member // 8) + rows_at // 8
    for g in range(2):
        col_ids = 16 * (member % 8) + 2 * (rows_at % 8) + g
        valid = jnp.logical_and(row_ids < height, col_ids < width)
        bias[g] = jnp.where(valid, 0.0, -jnp.inf).astype(F32)

    arrive(0)
    exchange(1)

    @pl.loop(0, 4)
    def _(i):
        tokens = split(came[0, pl.ds(pl.multiple_of(i * 128, 128), 128), :])
        for g in range(2):
            part = pl.ds(pl.multiple_of(g * MEMBERS + i * 64, 64), 64)
            centered = tokens[g] - jnp.mean(tokens[g], axis=-1, keepdims=True)
            scale = lax.rsqrt(jnp.mean(centered * centered, axis=-1, keepdims=True) + EPSILON)
            unit_rows = centered * scale
            unit[part, :] = unit_rows
            inv[part, :] = jnp.broadcast_to(scale, (64, 128))
            att[part, :] = unit_rows.astype(BF16)

    @pl.loop(0, 6)
    def _(i):
        part = pl.ds(pl.multiple_of(i * 128, 128), 128)
        normed_t[part, :] = att[:, part].T

    lane = lax.broadcasted_iota(jnp.int32, (MEMBERS, 128), 1) // HEAD_DIM
    to_exp2 = ROOT * math.log2(math.e)

    def one_head(value, j):
        return jnp.where(lane == j, value, jnp.zeros_like(value))

    def feature(i, size=128):
        return pl.ds(pl.multiple_of(i, size), size)

    def project(block):
        for n in range(3):
            tile = dot(att[...], weights[block, :, :, pl.ds(256 * n, 256)].reshape(D, 256)).astype(BF16)
            qkv[:, pl.ds(block * D + 256 * n, 256)] = tile
            if n > 0:
                kv_t[block, pl.ds(256 * (n - 1), 256), :] = tile.T

    def attend(block):
        @pl.loop(0, 4)
        def _(i):
            g, quad = i // 2, i % 2
            mine = feature(g * MEMBERS, MEMBERS)
            queries = qkv[mine, feature(block * D + quad * 128)]
            keys = qkv[mine, feature(block * D + 256 + quad * 128)]
            shift = bias[g]
            shift = jnp.concatenate([shift, shift], axis=1)
            for j in range(4):
                scores = dot_last(one_head(keys, j), queries) * to_exp2 + shift
                shifted = jnp.exp2(scores - jnp.max(scores, axis=0, keepdims=True))
                low = (shifted * (1.0 / jnp.sum(shifted, axis=0, keepdims=True))).astype(BF16)
                chances[(block * 4 + i) * 4 + j] = low
                values_t = kv_t[block, feature(256 + quad * 128 + j * 32, 32), mine]
                att_t[feature(block * 256 + quad * 128 + j * 32, 32), mine] = dot(values_t, low).astype(BF16)

    weights_there(0)
    project(0)
    project(1)
    attend(0)
    weights_core_far(1)
    attend(1)
    weights_there(1)
    project(2)
    attend(2)

    @pl.loop(0, 6)
    def _(i):
        part = feature(i * 128)
        att[:, part] = att_t[part, :].T

    for i in range(3):
        part = pl.ds(256 * i, 256)
        wide[:, part] = dot(att[...], weights[3, :, :, part].reshape(D, 256))

    @pl.loop(0, 4)
    def _(i):
        both = feature(i * 128)
        first = wide[feature(i * 64, 64), :]
        second = wide[feature(MEMBERS + i * 64, 64), :]
        sent[2, both, :] = (came[0, both, :].astype(F32) + merge(first, second)).astype(BF16)

    exchange(2)

    active = zl == x_at // 2
    owner = jnp.logical_and(active, zh < 3)
    mine48 = pl.ds(pl.multiple_of((x_at % 2) * 48, 16), 48)

    def start_core(b):
        push(
            terms.at[b, :, pl.ds(pl.multiple_of((1 - core) * HALF, 128), HALF)],
            core_in.at[b],
            r_send.at[b, 0],
            r_recv.at[b, 0],
            device(c=1 - core),
        )

    def start_y(b):
        wait(core_in.at[b], r_recv.at[b, 0])
        for l in range(2):
            for y in range(4):
                src, dst = pl.ds((l * 4 + y) * 96, 96), pl.ds((y * 2 + l) * 96, 96)
                cols = pl.ds(pl.multiple_of(core * HALF, 128), HALF)
                core_sum[b, dst, :] = (
                    terms[b, src, cols].astype(F32) + core_in[b, src, :].astype(F32)
                ).astype(BF16)

        for k in range(1, 4):
            y = (y_at + k) % 4
            src = core_sum.at[b, pl.ds(pl.multiple_of(y * 192, 16), 192)]
            push(src, y_in.at[b, k - 1], r_send.at[b, 1], r_recv.at[b, 1], device(y=y))

    def start_x(b):
        wait(y_in.at[b], r_recv.at[b, 1])
        acc = core_sum[b, pl.ds(pl.multiple_of(y_at * 192, 16), 192), :].astype(F32)
        for k in range(3):
            acc = acc + y_in[b, k].astype(F32)
        y_sum[b] = acc.astype(BF16)
        for k in range(1, 4):
            x = (x_at + k) % 4
            src = y_sum.at[b, pl.ds(pl.multiple_of(x * 48, 16), 48)]
            push(src, x_in.at[b, k - 1], r_send.at[b, 5], r_recv.at[b, 5], device(x=x))

    def start_z(b):
        wait(x_in.at[b], r_recv.at[b, 5])
        acc = y_sum[b, pl.ds(pl.multiple_of(x_at * 48, 16), 48), :].astype(F32)
        for k in range(3):
            acc = acc + x_in[b, k].astype(F32)
        x_sum[b] = acc.astype(BF16)
        for j in range(3):
            rows = pl.ds(16 * j, 16)

            @pl.when(jnp.logical_not(jnp.logical_and(active, zh == j)))
            def _():
                to = device(h=j, l=x_at // 2)
                push(x_sum.at[b, rows], z_in.at[b, zh * 2 + zl], r_send.at[b, 2], r_recv.at[b, 2], to)

            @pl.when(jnp.logical_and(active, zh == j))
            def _():
                z_in[b, zh * 2 + zl] = x_sum[b, rows, :]

    def start_regather(b):
        @pl.when(owner)
        def _():
            wait(z_in.at[b, pl.ds(0, 7)], r_recv.at[b, 2])
            acc = z_in[b, 0].astype(F32)
            for k in range(1, 8):
                acc = acc + z_in[b, k].astype(F32)
            rows = pl.ds(pl.multiple_of(zh * 16, 16), 16)
            total[b, rows, :] = acc.astype(BF16)
            for k in range(1, 4):
                to = device(h=(zh + k) % 4)
                push(total.at[b, rows], total.at[b, rows], r_send.at[b, 3], r_recv.at[b, 3], to)

    def start_spread(b):
        @pl.when(active)
        def _():
            @pl.when(zh < 3)
            def _():
                wait(total.at[b, pl.ds(0, 32)], r_recv.at[b, 3])

            @pl.when(zh == 3)
            def _():
                wait(total.at[b], r_recv.at[b, 3])

            for k in range(1, 8):
                to = device(x=(x_at + k // 2) % 4, c=(core + k) % 2)
                push(total.at[b], whole.at[b, core, mine48], r_send.at[b, 4], r_recv.at[b, 4], to)
            whole[b, core, mine48, :] = total[b]

    def finish_terms(b):
        @pl.when(active)
        def _():
            wait(core_in.at[b, pl.ds(0, 144)], r_recv.at[b, 4])

        @pl.when(jnp.logical_not(active))
        def _():
            wait(core_in.at[b, pl.ds(0, 192)], r_recv.at[b, 4])

        full = jnp.concatenate([whole[b, 0].astype(F32), whole[b, 1].astype(F32)], axis=1)
        if b == 0:
            wg_ref[:, pl.ds(3 * D, D)] = full
        else:
            for n in range(3):
                wg_ref[:, pl.ds(n * D + (b - 1) * 256, 256)] = full[:, n * 256 : (n + 1) * 256]

    def settle_terms(b):
        wait(core_in.at[b], r_send.at[b, 0])
        wait(y_in.at[b], r_send.at[b, 1])
        wait(x_in.at[b], r_send.at[b, 5])

        @pl.when(owner)
        def _():
            wait(z_in.at[b, pl.ds(0, 2)], r_send.at[b, 2])
            wait(z_in.at[b, pl.ds(0, 3)], r_send.at[b, 3])

        @pl.when(jnp.logical_not(owner))
        def _():
            wait(z_in.at[b, pl.ds(0, 3)], r_send.at[b, 2])

        @pl.when(active)
        def _():
            wait(core_in.at[b, pl.ds(0, 336)], r_send.at[b, 4])

    arrive(1)

    @pl.loop(0, 4)
    def _(i):
        grads = split(came[1, feature(i * 128), :])
        for g in range(2):
            part = feature(g * MEMBERS + i * 64, 64)
            keep = bias[g, feature(i * 64, 64), :] == 0.0
            keep = jnp.concatenate([keep.astype(F32)] * 6, axis=1)
            masked[part, :] = (grads[g] * keep).astype(BF16)

    for i in range(3):
        part = pl.ds(256 * i, 256)
        out_grad[:, part] = dot_last(masked[...], block_weights(3)[256 * i : 256 * i + 256]).astype(BF16)
    for i in range(3):
        part = pl.ds(256 * i, 256)
        terms[0, :, part] = dot(att_t[...], masked[:, part]).astype(BF16)
    start_core(0)

    def attend_back(block, g):
        @pl.loop(0, 2)
        def _(quad):
            mine = feature(g * MEMBERS, MEMBERS)
            queries = qkv[mine, feature(block * D + quad * 128)]
            values = qkv[mine, feature(block * D + 512 + quad * 128)]
            grads = out_grad[mine, feature(block * 256 + quad * 128)]
            key_grad = jnp.zeros((MEMBERS, 128), F32)
            value_grad = jnp.zeros((MEMBERS, 128), F32)
            query_grad = []
            for j in range(4):
                chance_grad = dot_last(one_head(values, j), grads)
                low = chances[(block * 4 + g * 2 + quad) * 4 + j]
                chance = low.astype(F32)
                spread = jnp.sum(chance * chance_grad, axis=0, keepdims=True)
                score_grad = (chance * (chance_grad - spread) * ROOT).astype(BF16)
                value_grad += dot(low, one_head(grads, j))
                key_grad += dot(score_grad, one_head(queries, j))
                keys_t = kv_t[block, feature(quad * 128 + j * 32, 32), mine]
                query_grad.append(dot(keys_t, score_grad))
            query_grad = jnp.concatenate(query_grad, axis=0).astype(BF16)
            proj_grad[mine, feature(block * D + quad * 128)] = query_grad.T
            proj_grad[mine, feature(block * D + 256 + quad * 128)] = key_grad.astype(BF16)
            proj_grad[mine, feature(block * D + 512 + quad * 128)] = value_grad.astype(BF16)

    def weight_terms(block):
        for n in range(3):
            cols = pl.ds(block * D + n * 256, 256)
            terms[block + 1, :, pl.ds(n * 256, 256)] = dot(normed_t[...], proj_grad[:, cols]).astype(BF16)

    attend_back(0, 0)
    start_y(0)
    attend_back(0, 1)
    weight_terms(0)
    start_core(1)
    attend_back(1, 0)
    start_x(0)
    start_y(1)
    attend_back(1, 1)
    weight_terms(1)
    start_core(2)
    start_z(0)
    attend_back(2, 0)
    start_x(1)
    start_y(2)
    start_regather(0)
    attend_back(2, 1)
    weight_terms(2)
    start_core(3)
    start_z(1)
    start_spread(0)
    for i in range(3):
        part = pl.ds(256 * i, 256)
        grad = jnp.zeros((TOKENS, 256), F32)
        for b in range(3):
            grad += dot_last(proj_grad[:, pl.ds(b * D, D)], block_weights(b)[256 * i : 256 * i + 256])
        wide[:, part] = grad
    start_y(3)
    start_x(2)

    @pl.loop(0, 4)
    def _(i):
        both = feature(i * 128)
        parts = []
        for g in range(2):
            part = feature(g * MEMBERS + i * 64, 64)
            grad, unit_rows = wide[part, :], unit[part, :]
            moved = (
                grad
                - jnp.mean(grad, axis=-1, keepdims=True)
                - unit_rows * jnp.mean(grad * unit_rows, axis=-1, keepdims=True)
            )
            scale = jnp.concatenate([inv[part, :]] * 6, axis=1)
            parts.append(masked[part, :].astype(F32) + scale * moved)
        sent[3, both, :] = merge(*parts).astype(BF16)

    start_regather(1)
    start_z(2)
    exchange(3, 0, 1, 8)
    exchange(3, 1, 8, 16)
    start_x(3)
    arrive(2)
    reorder(scatter, came.at[2], out_ref)
    start_spread(1)
    finish_terms(0)
    left(3, 0, 7)
    start_regather(2)
    start_z(3)
    exchange(3, 2, 16, 24)
    finish_terms(1)
    left(3, 1, 8)
    exchange(3, 3, 24, 32)
    start_spread(2)
    start_regather(3)
    finish_terms(2)
    start_spread(3)
    finish_terms(3)
    arrive(3)
    reorder(scatter, came.at[3], ig_ref)
    left(3, 2, 8)
    left(3, 3, 8)

    for t in range(4):
        if t < 3:
            left(t, 0, 31)
        settle_terms(t)
    for p in range(2):
        weights_settle(p)


def per_device(inputs, cotangent, extents, weights):
    shape = inputs.shape
    vmem = pl.BlockSpec(memory_space=pltpu.VMEM)
    out, ig, wg = pl.pallas_call(
        kernel,
        out_shape=(
            jax.ShapeDtypeStruct((TOKENS, D), BF16),
            jax.ShapeDtypeStruct((TOKENS, D), BF16),
            jax.ShapeDtypeStruct((96, 4 * D), F32),
        ),
        in_specs=[pl.BlockSpec(memory_space=pltpu.SMEM), vmem, vmem, vmem],
        out_specs=(vmem, vmem, vmem),
        scratch_shapes=[
            pltpu.VMEM((4, TOKENS, D), BF16),
            pltpu.VMEM((4, TOKENS, D), BF16),
            pltpu.VMEM((4, 8, 96, D), BF16),
            pltpu.VMEM((TOKENS, D), F32),
            pltpu.VMEM((TOKENS, 128), F32),
            pltpu.VMEM((D, TOKENS), BF16),
            pltpu.VMEM((TOKENS, 3 * D), BF16),
            pltpu.VMEM((3, TOKENS, TOKENS), BF16),
            pltpu.VMEM((2, MEMBERS, 128), F32),
            pltpu.VMEM((2 * HEADS, MEMBERS, MEMBERS), BF16),
            pltpu.VMEM((D, TOKENS), BF16),
            pltpu.VMEM((TOKENS, D), BF16),
            pltpu.VMEM((TOKENS, D), BF16),
            pltpu.VMEM((TOKENS, D), BF16),
            pltpu.VMEM((TOKENS, 3 * D), BF16),
            pltpu.VMEM((TOKENS, D), F32),
            pltpu.VMEM((4, D, D), BF16),
            pltpu.VMEM((4, D, HALF), BF16),
            pltpu.VMEM((4, D, HALF), BF16),
            pltpu.VMEM((4, 3, 192, HALF), BF16),
            pltpu.VMEM((4, 192, HALF), BF16),
            pltpu.VMEM((4, 3, 48, HALF), BF16),
            pltpu.VMEM((4, 48, HALF), BF16),
            pltpu.VMEM((4, 8, 16, HALF), BF16),
            pltpu.VMEM((4, 48, HALF), BF16),
            pltpu.VMEM((4, 2, 96, HALF), BF16),
            pltpu.SemaphoreType.DMA((4, 4)),
            pltpu.SemaphoreType.DMA((4,)),
            pltpu.SemaphoreType.DMA((2, 5)),
            pltpu.SemaphoreType.DMA((2, 5)),
            pltpu.SemaphoreType.DMA((4, 6)),
            pltpu.SemaphoreType.DMA((4, 6)),
        ],
        compiler_params=pltpu.CompilerParams(
            collective_id=0, has_side_effects=True, vmem_limit_bytes=60 << 20
        ),
    )(extents, inputs.reshape(TOKENS, D), cotangent.reshape(TOKENS, D), weights)
    return out.reshape(shape), ig.reshape(shape), wg


def solution(mesh):
    placed = (
        P("dp", "rows", None, None),
        P("dp", "rows", None, None),
        P("dp", None),
        P("dp", None),
    )
    return jax.shard_map(
        per_device,
        mesh=mesh,
        in_specs=placed,
        out_specs=(P("dp", "rows", None, None), P("dp", "rows", None, None), P("dp", None)),
        check_vma=False,
    )
```

time: 738 us -> 135 us (0.18); the launches traced: 728 us -> 134 us
  waiting for transfers between devices: 476 us -> 0 us
  Pallas kernels: 0 us -> 129 us
  matrix products: 86.4 us -> 0 us
  local copies, waits for them, and re-layouts: 84.3 us -> 4.1 us
  starting transfers between devices: 53.1 us -> 0 us
  between operations: 14.4 us -> 0.66 us
  other arithmetic: 13.4 us -> 0 us
    psum x1 -> x0, waiting for transfers between devices: 274 us -> none  [finish(): weight_grads = lax.psum(terms, 'rows').astype(jnp.float32)]
    pallas_call x0 -> x1, Pallas kernels: none -> 129 us  [per_device(): pl.pallas_call(kernel, out_shape=(jax.ShapeDtypeStruct((TOKENS, D), BF16)...]
    all_to_all x8 -> x0, waiting for transfers between devices: 96.4 us -> none  [the longest x1 22.4 us: per_device(): lax.all_to_all(send_out(projected[:, :width]), 'rows', split_axis=0, conc...]
    dot_general x11 -> x0, matrix products: 75.3 us -> none  [the longest x1 18.5 us: attend_back(): jnp.einsum('ghmn,gnhe->gmhe', score_grad, split_heads(key_vecs), preferre...]
    another operation x20 -> x0, local copies, waits for them, and re-layouts: 56.8 us -> none  [the longest x8 30.8 us: split_heads(): return values.reshape(group_count, members, HEADS, HEAD_DIM)]
    all_gather x1 -> x0, waiting for transfers between devices: 56.2 us -> none  [per_device(): full_weights = lax.all_gather(weights, 'dp', axis=0, tiled=True)]
    all_to_all x8 -> x0, starting transfers between devices: 52.7 us -> none  [the longest x1 9.95 us: per_device(): lax.all_to_all(regroup(key_grad), 'rows', split_axis=2, concat_axis=0, ti...]
    reduce_scatter x1 -> x0, waiting for transfers between devices: 48.4 us -> none  [finish(): lax.psum_scatter(jnp.concatenate([lax.dot_general(normed, proj_grad, cont...]
  transfers between devices with their start and end apart: 11 -> 0, of which waited for: 9 -> 0; matrix products, arithmetic and copies ran while one was open for 17% -> 0% of each run, Pallas kernels for 0% -> 0%
where the time goes in v1:
time: 135 us; the launch traced here: 134 us
  Pallas kernels  129 us (96%)
  local copies, waits for them, and re-layouts  4.1 us (3%)
    pallas_call x1, Pallas kernels, per_device(): pl.pallas_call(kernel, out_shape=(jax.ShapeDtypeStruct((TOKENS, D), BF16)...  129 us
    unnamed x7, local copies, waits for them, and re-layouts  4.1 us

profile of v1, /device:TPU:57, one launch (start us, length us, event | category | flops | bytes accessed | tf_op | source)
XLA Modules:
  0.0 133.9 jit_solution(14038516478104362231)
XLA Ops:
  0.6 129.2 %shard_map.67 = (bf16[512,768]{1,0:T(8,128)(2,1)}, bf16[512,768]{1,0:T(8,128)(2,1)}, f32[96,3072]{1,0:T(8,128)}) custom-call(s32[1,2]{1,0:T(1,128)} %extent_ref.1, bf16[512,768]{1,0:T(8,128)(2,1)} %bitcast.4, bf16[512,768]{1,0:T(8,128)(2,1)} %bitcast.5, bf16[96,3072]{1,0:T(8,128)(2,1)} %w_ref.1), custom_call_target="tpu_custom_call" | custom-call | tf_op jit(solution)/shard_map/pallas_call | solution.py:572
  129.8 0.0 copy-start.1
  129.8 0.0 copy-start
  129.8 2.2 %copy.10 = bf16[1,4,128,768]{3,2,1,0:T(8,128)(2,1)} copy(bf16[1,4,128,768]{3,2,1,0:T(8,128)(2,1)} %bitcast.7) | data formatting | bytes 1572864
  132.0 0.0 copy-done.1
  132.0 0.9 copy.11
  132.9 0.0 copy-done
  132.9 1.0 copy.12
Async XLA Ops:
  129.8 2.2 %copy-start.1 = (bf16[512,768]{1,0:T(8,128)(2,1)S(1)}, bf16[512,768]{1,0:T(8,128)(2,1)}, u32[]{:S(2)}) copy-start(bf16[512,768]{1,0:T(8,128)(2,1)} %get-tuple-element.7) | copy-start | bytes 2359300
  129.8 3.1 %copy-start = (f32[96,3072]{1,0:T(8,128)S(1)}, f32[96,3072]{1,0:T(8,128)}, u32[]{:S(2)}) copy-start(f32[96,3072]{1,0:T(8,128)} %get-tuple-element.14) | copy-start | bytes 3538948

commit v2 on v1

--- a/solution.py
+++ b/solution.py
@@ -73,6 +73,8 @@
     x_in,
     x_sum,
     z_in,
+    xy_in,
+    all_in,
     total,
     whole,
     a_send,
@@ -330,7 +332,7 @@
             device(c=1 - core),
         )
 
-    def start_y(b):
+    def add_core(b):
         wait(core_in.at[b], r_recv.at[b, 0])
         for l in range(2):
             for y in range(4):
@@ -340,6 +342,8 @@
                     terms[b, src, cols].astype(F32) + core_in[b, src, :].astype(F32)
                 ).astype(BF16)
 
+    def start_y(b):
+        add_core(b)
         for k in range(1, 4):
             y = (y_at + k) % 4
             src = core_sum.at[b, pl.ds(pl.multiple_of(y * 192, 16), 192)]
@@ -387,6 +391,51 @@
                 to = device(h=(zh + k) % 4)
                 push(total.at[b, rows], total.at[b, rows], r_send.at[b, 3], r_recv.at[b, 3], to)
 
+    def start_xy(b):
+        add_core(b)
+
+        @pl.loop(1, 16)
+        def _(k):
+            x, y = (x_at + k % 4) % 4, (y_at + k // 4) % 4
+            src = core_sum.at[b, pl.ds(pl.multiple_of(y * 192 + x * 48, 16), 48)]
+            push(src, xy_in.at[k - 1], r_send.at[b, 1], r_recv.at[b, 1], device(x=x, y=y))
+
+    def start_all(b):
+        wait(xy_in, r_recv.at[b, 1])
+        acc = core_sum[b, pl.ds(pl.multiple_of(y_at * 192 + x_at * 48, 16), 48), :].astype(F32)
+        for k in range(15):
+            acc = acc + xy_in[k].astype(F32)
+        low = acc.astype(BF16)
+        x_sum[b] = low
+        slot = all_in.at[zh * 2 + zl]
+        for k in range(1, 4):
+            to = device(h=(zh + k) % 4, l=x_at // 2)
+            push(x_sum.at[b], slot, r_send.at[b, 2], r_recv.at[b, 2], to)
+
+        @pl.when(jnp.logical_not(active))
+        def _():
+            push(x_sum.at[b], slot, r_send.at[b, 3], r_recv.at[b, 2], device(l=1 - zl))
+
+        @pl.when(active)
+        def _():
+            all_in[zh * 2 + zl] = low
+
+    def spread(b):
+        for k in range(1, 8):
+            to = device(x=(x_at + k // 2) % 4, c=(core + k) % 2)
+            push(total.at[b], whole.at[b, core, mine48], r_send.at[b, 4], r_recv.at[b, 4], to)
+        whole[b, core, mine48, :] = total[b]
+
+    def start_spread_all(b):
+        @pl.when(active)
+        def _():
+            wait(all_in.at[pl.ds(0, 7)], r_recv.at[b, 2])
+            acc = all_in[0].astype(F32)
+            for k in range(1, 8):
+                acc = acc + all_in[k].astype(F32)
+            total[b] = acc.astype(BF16)
+            spread(b)
+
     def start_spread(b):
         @pl.when(active)
         def _():
@@ -398,10 +447,7 @@
             def _():
                 wait(total.at[b], r_recv.at[b, 3])
 
-            for k in range(1, 8):
-                to = device(x=(x_at + k // 2) % 4, c=(core + k) % 2)
-                push(total.at[b], whole.at[b, core, mine48], r_send.at[b, 4], r_recv.at[b, 4], to)
-            whole[b, core, mine48, :] = total[b]
+            spread(b)
 
     def finish_terms(b):
         @pl.when(active)
@@ -412,7 +458,7 @@
         def _():
             wait(core_in.at[b, pl.ds(0, 192)], r_recv.at[b, 4])
 
-        full = jnp.concatenate([whole[b, 0].astype(F32), whole[b, 1].astype(F32)], axis=1)
+        full = jnp.concatenate([whole[b, 0], whole[b, 1]], axis=1)
         if b == 0:
             wg_ref[:, pl.ds(3 * D, D)] = full
         else:
@@ -421,17 +467,26 @@
 
     def settle_terms(b):
         wait(core_in.at[b], r_send.at[b, 0])
-        wait(y_in.at[b], r_send.at[b, 1])
-        wait(x_in.at[b], r_send.at[b, 5])
-
-        @pl.when(owner)
-        def _():
-            wait(z_in.at[b, pl.ds(0, 2)], r_send.at[b, 2])
-            wait(z_in.at[b, pl.ds(0, 3)], r_send.at[b, 3])
-
-        @pl.when(jnp.logical_not(owner))
-        def _():
-            wait(z_in.at[b, pl.ds(0, 3)], r_send.at[b, 2])
+        if b == 3:
+            wait(xy_in, r_send.at[b, 1])
+            wait(all_in.at[pl.ds(0, 3)], r_send.at[b, 2])
+
+            @pl.when(jnp.logical_not(active))
+            def _():
+                wait(x_sum.at[b], r_send.at[b, 3])
+
+        else:
+            wait(y_in.at[b], r_send.at[b, 1])
+            wait(x_in.at[b], r_send.at[b, 5])
+
+            @pl.when(owner)
+            def _():
+                wait(z_in.at[b, pl.ds(0, 2)], r_send.at[b, 2])
+                wait(z_in.at[b, pl.ds(0, 3)], r_send.at[b, 3])
+
+            @pl.when(jnp.logical_not(owner))
+            def _():
+                wait(z_in.at[b, pl.ds(0, 3)], r_send.at[b, 2])
 
         @pl.when(active)
         def _():
@@ -492,29 +547,26 @@
     weight_terms(0)
     start_core(1)
     attend_back(1, 0)
-    start_x(0)
     start_y(1)
     attend_back(1, 1)
     weight_terms(1)
     start_core(2)
+    start_x(0)
+    attend_back(2, 0)
+    start_y(2)
     start_z(0)
-    attend_back(2, 0)
-    start_x(1)
-    start_y(2)
-    start_regather(0)
     attend_back(2, 1)
     weight_terms(2)
     start_core(3)
-    start_z(1)
-    start_spread(0)
+    start_x(1)
     for i in range(3):
         part = pl.ds(256 * i, 256)
         grad = jnp.zeros((TOKENS, 256), F32)
         for b in range(3):
             grad += dot_last(proj_grad[:, pl.ds(b * D, D)], block_weights(b)[256 * i : 256 * i + 256])
         wide[:, part] = grad
-    start_y(3)
-    start_x(2)
+    start_xy(3)
+    start_regather(0)
 
     @pl.loop(0, 4)
     def _(i):
@@ -532,31 +584,28 @@
             parts.append(masked[part, :].astype(F32) + scale * moved)
         sent[3, both, :] = merge(*parts).astype(BF16)
 
-    start_regather(1)
-    start_z(2)
-    exchange(3, 0, 1, 8)
-    exchange(3, 1, 8, 16)
-    start_x(3)
+    start_x(2)
+    start_z(1)
+    exchange(3, 0, 1, 12)
     arrive(2)
     reorder(scatter, came.at[2], out_ref)
+    start_z(2)
+    start_spread(0)
+    start_regather(1)
+    start_all(3)
+    start_regather(2)
+    exchange(3, 1, 12, 32)
     start_spread(1)
     finish_terms(0)
-    left(3, 0, 7)
-    start_regather(2)
-    start_z(3)
-    exchange(3, 2, 16, 24)
+    start_spread(2)
+    start_spread_all(3)
     finish_terms(1)
-    left(3, 1, 8)
-    exchange(3, 3, 24, 32)
-    start_spread(2)
-    start_regather(3)
     finish_terms(2)
-    start_spread(3)
     finish_terms(3)
     arrive(3)
     reorder(scatter, came.at[3], ig_ref)
-    left(3, 2, 8)
-    left(3, 3, 8)
+    left(3, 0, 11)
+    left(3, 1, 20)
 
     for t in range(4):
         if t < 3:
@@ -574,7 +623,7 @@
         out_shape=(
             jax.ShapeDtypeStruct((TOKENS, D), BF16),
             jax.ShapeDtypeStruct((TOKENS, D), BF16),
-            jax.ShapeDtypeStruct((96, 4 * D), F32),
+            jax.ShapeDtypeStruct((96, 4 * D), BF16),
         ),
         in_specs=[pl.BlockSpec(memory_space=pltpu.SMEM), vmem, vmem, vmem],
         out_specs=(vmem, vmem, vmem),
@@ -603,9 +652,11 @@
             pltpu.VMEM((4, 3, 48, HALF), BF16),
             pltpu.VMEM((4, 48, HALF), BF16),
             pltpu.VMEM((4, 8, 16, HALF), BF16),
+            pltpu.VMEM((15, 48, HALF), BF16),
+            pltpu.VMEM((8, 48, HALF), BF16),
             pltpu.VMEM((4, 48, HALF), BF16),
             pltpu.VMEM((4, 2, 96, HALF), BF16),
-            pltpu.SemaphoreType.DMA((4, 4)),
+            pltpu.SemaphoreType.DMA((4, 2)),
             pltpu.SemaphoreType.DMA((4,)),
             pltpu.SemaphoreType.DMA((2, 5)),
             pltpu.SemaphoreType.DMA((2, 5)),
@@ -616,7 +667,7 @@
             collective_id=0, has_side_effects=True, vmem_limit_bytes=60 << 20
         ),
     )(extents, inputs.reshape(TOKENS, D), cotangent.reshape(TOKENS, D), weights)
-    return out.reshape(shape), ig.reshape(shape), wg
+    return out.reshape(shape), ig.reshape(shape), wg.astype(F32)
 
 
 def solution(mesh):

time: 135 us -> 133 us (0.985)
  other arithmetic: 0 us -> 2.25 us
  local copies, waits for them, and re-layouts: 4.1 us -> 2.3 us
    convert_element_type x0 -> x1, other arithmetic: none -> 2.25 us  [per_device(): return (out.reshape(shape), ig.reshape(shape), wg.astype(F32))]
    unnamed x7 -> x6, local copies, waits for them, and re-layouts: 4.1 us -> 2.3 us
    pallas_call x1, Pallas kernels: 129 us -> 128 us  [per_device(): pl.pallas_call(kernel, out_shape=(jax.ShapeDtypeStruct((TOKENS, D), BF16)...]
where the time goes in v2:
time: 133 us
  Pallas kernels  128 us (96%)
  local copies, waits for them, and re-layouts  2.3 us (2%)
  other arithmetic  2.25 us (2%)
    pallas_call x1, Pallas kernels, per_device(): pl.pallas_call(kernel, out_shape=(jax.ShapeDtypeStruct((TOKENS, D), BF16)...  128 us

profile of v2, /device:TPU:57, one launch (start us, length us, event | category | flops | bytes accessed | tf_op | source)
XLA Modules:
  0.0 132.8 jit_solution(13408784090016621815)
XLA Ops:
  0.6 127.6 %shard_map.67 = (bf16[512,768]{1,0:T(8,128)(2,1)}, bf16[512,768]{1,0:T(8,128)(2,1)}, bf16[96,3072]{1,0:T(8,128)(2,1)}) custom-call(s32[1,2]{1,0:T(1,128)} %extent_ref.1, bf16[512,768]{1,0:T(8,128)(2,1)} %bitcast.4, bf16[512,768]{1,0:T(8,128)(2,1)} %bitcast.5, bf16[96,3072]{1,0:T(8,128)(2,1)} %w_ref.1), custom_call_target="tpu_custom_call" | custom-call | tf_op jit(solution)/shard_map/pallas_call | solution.py:621
  128.2 0.0 copy-start.1
  128.2 2.2 %convert_element_type.3 = f32[96,3072]{1,0:T(8,128)} convert(bf16[96,3072]{1,0:T(8,128)(2,1)} %get-tuple-element.8) | non-fusion elementwise | flops 294912 | bytes 1769472 | tf_op jit(solution)/shard_map/convert_element_type | solution.py:670
  130.5 0.0 copy-done.1
  130.5 0.0 copy-start
  130.5 0.9 copy.9
  131.4 0.5 copy-done
  131.9 0.9 copy.10
Async XLA Ops:
  128.2 2.3 %copy-start.1 = (bf16[512,768]{1,0:T(8,128)(2,1)S(1)}, bf16[512,768]{1,0:T(8,128)(2,1)}, u32[]{:S(2)}) copy-start(bf16[512,768]{1,0:T(8,128)(2,1)} %get-tuple-element.6) | copy-start | bytes 2359300
  130.5 1.4 %copy-start = (bf16[512,768]{1,0:T(8,128)(2,1)S(1)}, bf16[512,768]{1,0:T(8,128)(2,1)}, u32[]{:S(2)}) copy-start(bf16[512,768]{1,0:T(8,128)(2,1)} %get-tuple-element.7) | copy-start | bytes 2359300

commit v3 on v2

--- a/solution.py
+++ b/solution.py
@@ -226,8 +226,8 @@
     weights_near(1)
     reorder(gather, g_ref, sent.at[1])
     weights_core_near(0)
+    weights_core_far(0)
     weights_across(1)
-    weights_core_far(0)
     weights_core_near(1)
 
     height, width = extent_ref[0, 0], extent_ref[0, 1]

time: 133 us -> 132 us (level)
  the two profiles are of different devices: /device:TPU:57 before, /device:TPU:5 now
where the time goes in v3:
time: 132 us
  Pallas kernels  127 us (96%)
  local copies, waits for them, and re-layouts  2.3 us (2%)
  other arithmetic  2.25 us (2%)
    pallas_call x1, Pallas kernels, per_device(): pl.pallas_call(kernel, out_shape=(jax.ShapeDtypeStruct((TOKENS, D), BF16)...  127 us

profile of v3, /device:TPU:5, one launch (start us, length us, event | category | flops | bytes accessed | tf_op | source)
XLA Modules:
  0.0 131.9 jit_solution(4439512442005846043)
XLA Ops:
  0.6 126.7 %shard_map.67 = (bf16[512,768]{1,0:T(8,128)(2,1)}, bf16[512,768]{1,0:T(8,128)(2,1)}, bf16[96,3072]{1,0:T(8,128)(2,1)}) custom-call(s32[1,2]{1,0:T(1,128)} %extent_ref.1, bf16[512,768]{1,0:T(8,128)(2,1)} %bitcast.4, bf16[512,768]{1,0:T(8,128)(2,1)} %bitcast.5, bf16[96,3072]{1,0:T(8,128)(2,1)} %w_ref.1), custom_call_target="tpu_custom_call" | custom-call | tf_op jit(solution)/shard_map/pallas_call | solution.py:621
  127.3 0.0 copy-start.1
  127.3 2.2 %convert_element_type.3 = f32[96,3072]{1,0:T(8,128)} convert(bf16[96,3072]{1,0:T(8,128)(2,1)} %get-tuple-element.8) | non-fusion elementwise | flops 294912 | bytes 1769472 | tf_op jit(solution)/shard_map/convert_element_type | solution.py:670
  129.6 0.0 copy-done.1
  129.6 0.0 copy-start
  129.6 0.9 copy.9
  130.4 0.5 copy-done
  131.0 0.9 copy.10
Async XLA Ops:
  127.3 2.3 %copy-start.1 = (bf16[512,768]{1,0:T(8,128)(2,1)S(1)}, bf16[512,768]{1,0:T(8,128)(2,1)}, u32[]{:S(2)}) copy-start(bf16[512,768]{1,0:T(8,128)(2,1)} %get-tuple-element.6) | copy-start | bytes 2359300
  129.6 1.4 %copy-start = (bf16[512,768]{1,0:T(8,128)(2,1)S(1)}, bf16[512,768]{1,0:T(8,128)(2,1)}, u32[]{:S(2)}) copy-start(bf16[512,768]{1,0:T(8,128)(2,1)} %get-tuple-element.7) | copy-start | bytes 2359300
